TPU v7x, 32 devices: a whole 2x2x4 slice. The times are simulated.
32 devices in a mesh: ctx: 16 (over z, y, x), fsdp: 2 (over core).
Axes of the slice: x: 2, y: 2, z: 4, core: 2. Of those that a mesh axis runs over, the one named last changes fastest.
Arguments:
- tokens: bfloat16 [2, 4096, 1024], P('fsdp', 'ctx'), may hold values from -6 to 6
- cotangent: bfloat16 [2, 4096, 1024], P('fsdp', 'ctx'), may hold values from -6 to 6
- sequence_adapter_index: int32 [2], P('fsdp'), may hold values from 0 to 1, as said below
- query_key_value_weight: bfloat16 [1024, 3072], P('fsdp'), may hold values from -0.1875 to 0.1875
- output_weight: bfloat16 [1024, 1024], P('fsdp'), may hold values from -6 to 6
- first_feed_weight: bfloat16 [1024, 4096], P('fsdp'), may hold values from -0.1875 to 0.1875
- second_feed_weight: bfloat16 [4096, 1024], P('fsdp'), may hold values from -0.09375 to 0.09375
- biases: float32 [5, 1024], replicated, may hold values from -1.25 to 1.25
- value_bias_vector: float32 [1024], replicated, may hold values from -0.0625 to 0.0625
- first_feed_bias: float32 [4096], replicated, may hold values from -1.25 to 1.25
- norm_gain_pair: float32 [2, 1024], replicated, may hold values from 0.5 to 1.5
- adapter_down_factors: bfloat16 [8, 4, 16, 1024], replicated, may hold values from -0.1875 to 0.1875
- output_down_factor: bfloat16 [8, 16, 1024], replicated, may hold values from -6 to 6
- adapter_up_factors: bfloat16 [8, 5, 16, 1024], replicated, may hold values from -0.75 to 0.75
- hidden_up_factor: bfloat16 [8, 16, 4096], replicated, may hold values from -0.75 to 0.75
- hidden_down_factor: bfloat16 [8, 16, 4096], replicated, may hold values from -0.09375 to 0.09375
Outputs:
- outcome: bfloat16 [2, 4096, 1024], P('fsdp', 'ctx')
- grad_tokens: float32 [2, 4096, 1024], P('fsdp', 'ctx')
- grad_lora_down: float32 [8, 4, 16, 1024], replicated
- grad_lora_out_down: float32 [8, 16, 1024], replicated
- grad_lora_up: float32 [8, 5, 16, 1024], replicated
- grad_hid_up: float32 [8, 16, 4096], replicated
- grad_hid_down: float32 [8, 16, 4096], replicated
Inputs may be any that keep to these rules, and one draw needn't show every extreme that they name: `sequence_adapter_index`: each of the values 0 .. min(8, 2) - 1 is used by the same number of sequences: 0 where 2 is 8 or more, else one.
All inputs are finite; a program needn't handle non-finite values.
Results may differ from a plain program's by a relative error of at most 0.023.
Values may be sent and summed in bfloat16 or wider, within the bound.
A program may use at most 256 MiB of HBM per device.

v0:
```python
import functools

import jax
import jax.numpy as jnp
from jax import lax
from jax.experimental import pallas as pl
from jax.experimental.pallas import tpu as pltpu
from jax.sharding import PartitionSpec as P

H = 16


EPSILON = 1e-05
HIGHEST = lax.Precision.HIGHEST


def exact_sum(form, left, right):
    return jnp.einsum(form, left, right, precision=HIGHEST, preferred_element_type=jnp.float32)


def plain_sum(form, left, right):
    return jnp.einsum(form, left, right, preferred_element_type=jnp.float32)


def layer_norm(value, gain, shift):
    center = value - jnp.mean(value, -1, keepdims=True)
    spread = jnp.mean(center * center, -1, keepdims=True)
    return center * lax.rsqrt(spread + EPSILON) * gain + shift


def attn_weights(query_key_value_weight, output_weight):
    return (
        lax.all_gather(query_key_value_weight, "fsdp", axis=0, tiled=True),
        lax.all_gather(output_weight, "fsdp", axis=0, tiled=True),
    )


def mlp_weights(first_feed_weight, second_feed_weight):
    return (
        lax.all_gather(first_feed_weight, "fsdp", axis=0, tiled=True),
        lax.all_gather(second_feed_weight, "fsdp", axis=0, tiled=True),
    )


def to_heads(input_array):
    return input_array.reshape(
        input_array.shape[0], input_array.shape[1], H, input_array.shape[2] // H
    )


def row_block(input_array, block_index, block_rows):
    return lax.dynamic_slice_in_dim(input_array, block_index * block_rows, block_rows, 1)


def block_grads(queries, grad_out, log_total, row_delta, keys_blk, values_blk):
    scores = plain_sum("sqhd,skhd->shqk", queries, keys_blk)
    probs = jnp.exp(scores - log_total[..., None])
    prob_low = probs.astype(jnp.bfloat16)
    grad_probs = plain_sum("sqhd,skhd->shqk", grad_out, values_blk)
    grad_scores = (probs * (grad_probs - row_delta[..., None])).astype(jnp.bfloat16)
    return (prob_low, grad_scores)


def attention_forward(queries_heads, keys_heads, values_heads):
    seq_count, row_count, head_count, head_size = queries_heads.shape
    length = keys_heads.shape[1]
    block_rows = min(512, length)
    block_count = length // block_rows

    def max_step(running, block_index):
        running_max, running_total = running
        scores = plain_sum(
            "sqhd,skhd->shqk", queries_heads, row_block(keys_heads, block_index, block_rows)
        )
        new_max = jnp.maximum(running_max, jnp.max(scores, -1))
        running_total = running_total * jnp.exp(running_max - new_max) + jnp.sum(
            jnp.exp(scores - new_max[..., None]), -1
        )
        return ((new_max, running_total), None)

    start_max = jnp.full((seq_count, head_count, row_count), -1e30, jnp.float32)
    start_total = jnp.zeros((seq_count, head_count, row_count), jnp.float32)
    (final_max, final_total), unused = lax.scan(
        max_step, (start_max, start_total), jnp.arange(block_count)
    )
    log_total = final_max + jnp.log(final_total)

    def value_step(running, block_index):
        scores = plain_sum(
            "sqhd,skhd->shqk", queries_heads, row_block(keys_heads, block_index, block_rows)
        )
        prob_low = jnp.exp(scores - log_total[..., None]).astype(jnp.bfloat16)
        return (
            running
            + plain_sum(
                "shqk,skhd->sqhd", prob_low, row_block(values_heads, block_index, block_rows)
            ),
            None,
        )

    context, unused = lax.scan(
        value_step, jnp.zeros(queries_heads.shape, jnp.float32), jnp.arange(block_count)
    )
    return (context, log_total)


def gather_body(
    tokens,
    cotangent,
    sequence_adapter_index,
    query_key_value_weight,
    output_weight,
    first_feed_weight,
    second_feed_weight,
    biases,
    value_bias_vector,
    first_feed_bias,
    norm_gain_pair,
    adapter_down_factors,
    output_down_factor,
    adapter_up_factors,
    hidden_up_factor,
    hidden_down_factor,
):
    seq_count, row_count, model_width = tokens.shape
    adapter_number = adapter_down_factors.shape[0]
    picker = (
        sequence_adapter_index[:, None] == jnp.arange(adapter_number, dtype=jnp.int32)[None, :]
    ).astype(jnp.float32)

    def select_adapter(table):
        return jnp.einsum("sa,a...->s...", picker, table.astype(jnp.float32), precision=HIGHEST)

    def to_adapters(per_seq):
        return jnp.einsum("sa,s...->a...", picker, per_seq, precision=HIGHEST)

    selected_down = select_adapter(adapter_down_factors)
    selected_output = select_adapter(output_down_factor)
    selected_up = select_adapter(adapter_up_factors)
    hup_sel = select_adapter(hidden_up_factor)
    hdown_sel = select_adapter(hidden_down_factor)
    down_low = selected_down.astype(jnp.bfloat16)
    out_low = selected_output.astype(jnp.bfloat16)
    hdown_low = hdown_sel.astype(jnp.bfloat16)
    wqkv_full, wout_full = attn_weights(query_key_value_weight, output_weight)
    projected = plain_sum("std,de->ste", tokens, wqkv_full)
    down_att = plain_sum("std,sjrd->sjtr", tokens, down_low[:, :3])
    lifted = exact_sum("sjtr,sjrd->sjtd", down_att, selected_up[:, :3])
    queries = ((projected[..., :model_width] + biases[0] + lifted[:, 0]) * 0.125).astype(
        jnp.bfloat16
    )
    keys_own = (projected[..., model_width : 2 * model_width] + lifted[:, 1]).astype(jnp.bfloat16)
    values_own = (projected[..., 2 * model_width :] + value_bias_vector + lifted[:, 2]).astype(
        jnp.bfloat16
    )
    keys_all, values_all = (
        lax.all_gather(keys_own, "ctx", axis=1, tiled=True),
        lax.all_gather(values_own, "ctx", axis=1, tiled=True),
    )
    queries_heads = to_heads(queries)
    keys_heads = to_heads(keys_all)
    values_heads = to_heads(values_all)
    context, log_total = attention_forward(queries_heads, keys_heads, values_heads)
    context = context.reshape(seq_count, row_count, model_width)
    context_low = context.astype(jnp.bfloat16)
    down_out = plain_sum("std,srd->str", context_low, out_low)
    branch = (
        plain_sum("std,de->ste", context_low, wout_full)
        + biases[1]
        + exact_sum("str,srd->std", down_out, selected_up[:, 3])
    )

    def first_norm(value):
        return layer_norm(value, norm_gain_pair[0], biases[3])

    def second_norm(value):
        return layer_norm(value, norm_gain_pair[1], biases[4])

    def gelu_exact(value):
        return jax.nn.gelu(value, approximate=False)

    normed, norm_back = jax.vjp(first_norm, tokens.astype(jnp.float32) + branch)
    normed_low = normed.astype(jnp.bfloat16)
    wfc1_full, wfc2_full = mlp_weights(first_feed_weight, second_feed_weight)
    down_fc1 = plain_sum("std,srd->str", normed_low, down_low[:, 3])
    hidden_pre = (
        plain_sum("std,df->stf", normed_low, wfc1_full)
        + first_feed_bias
        + exact_sum("str,srf->stf", down_fc1, hup_sel)
    )
    activated, gelu_back = jax.vjp(gelu_exact, hidden_pre)
    act_low = activated.astype(jnp.bfloat16)
    down_fc2 = plain_sum("stf,srf->str", act_low, hdown_low)
    mixed_out = (
        plain_sum("stf,fd->std", act_low, wfc2_full)
        + biases[2]
        + exact_sum("str,srd->std", down_fc2, selected_up[:, 4])
    )
    outcome, out_back = jax.vjp(second_norm, normed + mixed_out)
    (grad_sum2,) = out_back(cotangent.astype(jnp.float32))
    grad_mixed = grad_sum2.astype(jnp.bfloat16)
    grad_up_fc2 = exact_sum("str,std->srd", down_fc2, grad_mixed)
    grad_rank_fc2 = exact_sum("std,srd->str", grad_mixed, selected_up[:, 4]).astype(jnp.bfloat16)
    grad_hdown = plain_sum("str,stf->srf", grad_rank_fc2, act_low)
    wfc1_full, wfc2_full = mlp_weights(first_feed_weight, second_feed_weight)
    grad_act = (
        plain_sum("std,fd->stf", grad_mixed, wfc2_full)
        + plain_sum("str,srf->stf", grad_rank_fc2, hdown_low)
    ).astype(jnp.bfloat16)
    (grad_hidden,) = gelu_back(grad_act.astype(jnp.float32))
    grad_hidden = grad_hidden.astype(jnp.bfloat16)
    grad_hup = exact_sum("str,stf->srf", down_fc1, grad_hidden)
    grad_rank_fc1 = exact_sum("stf,srf->str", grad_hidden, hup_sel).astype(jnp.bfloat16)
    grad_down_fc1 = plain_sum("str,std->srd", grad_rank_fc1, normed_low)
    grad_normed_low = (
        plain_sum("stf,df->std", grad_hidden, wfc1_full)
        + plain_sum("str,srd->std", grad_rank_fc1, down_low[:, 3])
    ).astype(jnp.bfloat16)
    (grad_resid,) = norm_back(grad_sum2 + grad_normed_low.astype(jnp.float32))
    mlp_hup = to_adapters(grad_hup)
    mlp_hdown = to_adapters(grad_hdown)
    mlp_fc1 = to_adapters(grad_down_fc1)
    mlp_fc2 = to_adapters(grad_up_fc2)
    mlp_hup, mlp_hdown, mlp_fc1, mlp_fc2 = lax.psum(
        (mlp_hup, mlp_hdown, mlp_fc1, mlp_fc2), ("ctx", "fsdp")
    )
    grad_branch = grad_resid.astype(jnp.bfloat16)
    grad_up_out = exact_sum("str,std->srd", down_out, grad_branch)
    grad_rank_out = exact_sum("std,srd->str", grad_branch, selected_up[:, 3]).astype(jnp.bfloat16)
    grad_out_down = plain_sum("str,std->srd", grad_rank_out, context_low)
    wqkv_full, wout_full = attn_weights(query_key_value_weight, output_weight)
    grad_context = (
        plain_sum("std,ed->ste", grad_branch, wout_full)
        + plain_sum("str,srd->std", grad_rank_out, out_low)
    ).astype(jnp.bfloat16)
    row_delta = jnp.sum(to_heads(grad_context.astype(jnp.float32) * context), -1)
    delta_heads = jnp.swapaxes(row_delta, 1, 2)
    grad_heads = to_heads(grad_context)
    length = keys_all.shape[1]
    block_rows = min(512, length)
    block_count = length // block_rows

    def key_step(block_index, running):
        grad_query, grad_key, grad_value = running
        keys_blk = row_block(keys_heads, block_index, block_rows)
        values_blk = row_block(values_heads, block_index, block_rows)
        prob_low, grad_scores = block_grads(
            queries_heads, grad_heads, log_total, delta_heads, keys_blk, values_blk
        )
        grad_query = grad_query + plain_sum("shqk,skhd->sqhd", grad_scores, keys_blk)
        grad_key = lax.dynamic_update_slice_in_dim(
            grad_key,
            plain_sum("shqk,sqhd->skhd", grad_scores, queries_heads),
            block_index * block_rows,
            1,
        )
        grad_value = lax.dynamic_update_slice_in_dim(
            grad_value,
            plain_sum("shqk,sqhd->skhd", prob_low, grad_heads),
            block_index * block_rows,
            1,
        )
        return (grad_query, grad_key, grad_value)

    start_query = jnp.zeros(queries_heads.shape, jnp.float32)
    start_keys = jnp.zeros(keys_heads.shape, jnp.float32)
    grad_query, grad_key_all, grad_value_all = lax.fori_loop(
        0, block_count, key_step, (start_query, start_keys, start_keys)
    )
    grad_keys, grad_values = (
        lax.psum_scatter(
            grad_key_all.reshape(seq_count, length, model_width).astype(jnp.bfloat16),
            "ctx",
            scatter_dimension=1,
            tiled=True,
        ).astype(jnp.float32),
        lax.psum_scatter(
            grad_value_all.reshape(seq_count, length, model_width).astype(jnp.bfloat16),
            "ctx",
            scatter_dimension=1,
            tiled=True,
        ).astype(jnp.float32),
    )
    grad_qlin = grad_query.reshape(seq_count, row_count, model_width).astype(jnp.bfloat16) * 0.125
    grad_key_low = grad_keys.astype(jnp.bfloat16)
    grad_value_low = grad_values.astype(jnp.bfloat16)
    stacked = jnp.stack([grad_qlin, grad_key_low, grad_value_low], 1)
    grad_up_att = exact_sum("sjtr,sjtd->sjrd", down_att, stacked)
    grad_rank_att = exact_sum("sjtd,sjrd->sjtr", stacked, selected_up[:, :3]).astype(jnp.bfloat16)
    grad_down_att = plain_sum("sjtr,std->sjrd", grad_rank_att, tokens)
    joined = jnp.concatenate([grad_qlin, grad_key_low, grad_value_low], -1)
    grad_tokens = (
        grad_resid
        + plain_sum("ste,de->std", joined, wqkv_full)
        + plain_sum("sjtr,sjrd->std", grad_rank_att, down_low[:, :3])
    )
    attn_down = to_adapters(grad_down_att)
    attn_out = to_adapters(grad_out_down)
    attn_up = to_adapters(jnp.concatenate([grad_up_att, grad_up_out[:, None]], 1))
    attn_down, attn_out, attn_up = lax.psum((attn_down, attn_out, attn_up), ("ctx", "fsdp"))
    total_down = jnp.concatenate([attn_down, mlp_fc1[:, None]], 1)
    total_up = jnp.concatenate([attn_up, mlp_fc2[:, None]], 1)
    return (
        outcome.astype(jnp.bfloat16),
        grad_tokens,
        total_down,
        attn_out,
        total_up,
        mlp_hup,
        mlp_hdown,
    )


BF16 = jnp.bfloat16
F32 = jnp.float32
LOG2E = 1.4426950408889634
VMEM_LIMIT = 60 * 2**20
MESH = pl.DeviceIdType.MESH


def dot32(left, right):
    return jnp.dot(left, right, preferred_element_type=F32)


def dot_nt(left, right):
    return lax.dot_general(left, right, (((1,), (1,)), ((), ())), preferred_element_type=F32)


def dot_tn(left, right):
    return lax.dot_general(left, right, (((0,), (0,)), ((), ())), preferred_element_type=F32)


def split_three(value):
    high = value.astype(BF16)
    rest = value - high.astype(F32)
    middle = rest.astype(BF16)
    return high, middle, (rest - middle.astype(F32)).astype(BF16)


def flip(value):
    return value.astype(F32).T.astype(BF16)


def remote(src, dst, send_sem, recv_sem, device):
    return pltpu.make_async_remote_copy(
        src_ref=src,
        dst_ref=dst,
        send_sem=send_sem,
        recv_sem=recv_sem,
        device_id=device,
        device_id_type=MESH,
    )


class Place:
    def __init__(self):
        self.ctx = lax.axis_index("ctx")
        self.core = lax.axis_index("fsdp")
        self.half = self.ctx // (H // 2)
        self.low = self.ctx % (H // 2)
        self.me = self.low * 2 + self.core
        self.swaps = self.core != self.half
        self.pair = (self.core + self.half) % 2
        self.sibling = (self.ctx, 1 - self.core)
        self.partner = ((self.ctx + H // 2) % H, 1 - self.core)

    def peer(self, step):
        number = self.me ^ step
        return (self.half * (H // 2) + number // 2, number % 2)

    def order(self, turn):
        return 2 * (turn % (H // 2)) + (turn // (H // 2) + self.pair) % 2

    def greet(self):
        barrier = pltpu.get_barrier_semaphore()
        for step in range(1, H):
            pl.semaphore_signal(barrier, inc=1, device_id=self.peer(step), device_id_type=MESH)
        pl.semaphore_signal(barrier, inc=1, device_id=self.partner, device_id_type=MESH)
        pl.semaphore_wait(barrier, H)


def sum_copies(mine, parts, total, sems, place):
    own = total.at[place.pair, place.low, place.half]
    other = total.at[place.pair, place.low, 1 - place.half]
    column = total.at[place.pair]
    scatter = [
        remote(mine.at[place.me ^ step], parts.at[step], sems.at[0, step], sems.at[1, step], place.peer(step))
        for step in range(1, H)
    ]
    cross = remote(own, own, sems.at[0, 0], sems.at[1, 0], place.partner)
    first = [
        remote(own, own, sems.at[2, step], sems.at[3, step], place.peer(step))
        for step in range(2, H, 2)
    ]
    second = [
        remote(other, other, sems.at[2, step + 1], sems.at[3, step + 1], place.peer(step))
        for step in range(2, H, 2)
    ]
    last = remote(column, column, sems.at[2, 0], sems.at[3, 0], place.sibling)
    return scatter, cross, first, second, last


def sum_parts(scatter, mine, parts, total, place):
    value = mine[place.me].astype(F32)
    for step, copy in enumerate(scatter, 1):
        copy.wait_recv()
        value = value + parts[step].astype(F32)
    total[place.pair, place.low, place.half] = value.astype(BF16)


def put_term(mine, base, term):
    units = mine.shape[2] // 128
    for unit in range(term.shape[1] // 128):
        at = base // 128 + unit
        lanes = slice(at % units * 128, at % units * 128 + 128)
        mine[at // units, :, lanes] = term[:, unit * 128 : unit * 128 + 128].astype(BF16)


def layer_kernel(
    block_q,
    block_k,
    index_ref,
    tokens_ref,
    cotangent_ref,
    wqkv_ref,
    wout_ref,
    wfc1_ref,
    wfc2_ref,
    down_table,
    up_table,
    out_down_table,
    hidden_up_table,
    hidden_down_table,
    biases_ref,
    value_bias_ref,
    hidden_bias_ref,
    gains_ref,
    outcome_ref,
    grad_ref,
    chosen_out,
    hidden_down_out,
    hidden_up_out,
    down_out,
    up_out,
    out_down_out,
    wqkv_far,
    wfc1_far,
    wide,
    wfc2,
    wout,
    big,
    act,
    small,
    small_hidden,
    x,
    cotangent,
    rank_att,
    outgoing,
    qkv,
    leaving,
    arrived,
    incoming,
    context,
    state,
    qta,
    gta,
    kk,
    vv,
    kt,
    both,
    dkv_sum,
    dq_in,
    dkv_out,
    dkv_in,
    grad_out,
    grad_in,
    mlp_mine,
    mlp_parts,
    mlp_total,
    att_mine,
    att_parts,
    att_total,
    load_sem,
    core_sem,
    swap_sem,
    kv_sem,
    q_sem,
    back_sem,
    grad_sem,
    dq_sem,
    dkv_sem,
    mlp_sem,
    att_sem,
):
    peers, _, rows = qkv.shape
    length = peers * rows
    width = x.shape[1]
    hidden = hidden_bias_ref.shape[1]
    adapters = hidden_up_table.shape[0] // 16
    place = Place()
    me, core = place.me, place.core
    other = 1 - core
    wqkv = wide.at[:, 0 : 3 * width]
    up_at = down_table.shape[0]
    out_down_at = up_at + up_table.shape[0]

    def half_of(full, owner):
        count = full.shape[0] // 2
        return full.at[pl.ds(pl.multiple_of(owner * count, count), count), :]

    def load(source, target, number):
        return pltpu.make_async_copy(source, target, load_sem.at[number])

    def to_sibling(source, target, number):
        return remote(source, target, core_sem.at[0, number], core_sem.at[1, number], place.sibling)

    load_wqkv = load(wqkv_ref, half_of(wqkv, core), 0)
    load_wout = load(wout_ref, half_of(wout, core), 1)
    load_tables = [
        load(down_table, wfc2.at[0:up_at], 2),
        load(up_table, wfc2.at[up_at:out_down_at], 3),
        load(out_down_table, wfc2.at[out_down_at : out_down_at + out_down_table.shape[0]], 4),
        load(hidden_up_table, act.at[0 : 16 * adapters], 5),
        load(hidden_down_table, act.at[16 * adapters : 32 * adapters], 6),
    ]
    load_x = load(tokens_ref, x, 7)
    load_cotangent = load(cotangent_ref, cotangent, 8)
    load_wfc1 = load(wfc1_ref, half_of(wide, core), 9)
    load_wfc1_far = load(wfc1_far, half_of(wide, other), 10)
    load_wfc2 = load(wfc2_ref, half_of(wfc2, core), 11)
    again_wqkv = load(wqkv_ref, half_of(wqkv, core), 12)
    again_wqkv_far = load(wqkv_far, half_of(wqkv, other), 13)
    give_wqkv = to_sibling(wqkv_ref, half_of(wqkv, core), 0)
    give_wout = to_sibling(wout_ref, half_of(wout, core), 1)
    give_chosen = to_sibling(chosen_out.at[core], chosen_out.at[core], 2)
    count = small.shape[0]
    give_small = [to_sibling(small, wide.at[0:count, 3 * width : 4 * width], 3)] + [
        to_sibling(
            small_hidden.at[:, part * width : (part + 1) * width],
            wide.at[count + 32 * part : count + 32 * part + 32, 3 * width : 4 * width],
            4 + part,
        )
        for part in range(hidden // width)
    ]
    give_wfc2 = to_sibling(wfc2_ref, half_of(wfc2, core), 8)
    give_wfc1 = to_sibling(wfc1_ref, wfc1_far, 9)
    give_wqkv_again = to_sibling(wqkv_ref, wqkv_far, 10)
    half_rows = rows // 2
    swap_x = [
        remote(
            tokens_ref.at[part * half_rows : (part + 1) * half_rows],
            x.at[part * half_rows : (part + 1) * half_rows],
            swap_sem.at[0, 7 + part],
            swap_sem.at[1, 7 + part],
            place.partner,
        )
        for part in range(2)
    ]
    swap_cotangent = remote(cotangent_ref, cotangent, swap_sem.at[0, 1], swap_sem.at[1, 1], place.partner)

    load_wqkv.start()
    for copy in load_tables:
        copy.start()
    load_wout.start()

    @pl.when(jnp.logical_not(place.swaps))
    def _():
        load_x.start()
        load_cotangent.start()

    adapter = index_ref[0]
    numbers = lax.broadcasted_iota(jnp.int32, chosen_out.shape[1:], 0)
    chosen_out[core] = (numbers == jnp.full(numbers.shape, adapter, jnp.int32)).astype(F32)
    place.greet()

    @pl.when(place.swaps)
    def _():
        for copy in swap_x:
            copy.start()

    give_wqkv.start()
    give_chosen.start()

    for copy in load_tables:
        copy.wait()

    def select(table, base, group, groups, target, at):
        chosen = jnp.full((16, table.shape[1]), adapter, jnp.int32)
        value = jnp.zeros((16, table.shape[1]), F32)
        for number in range(adapters):
            start = pl.multiple_of(base + 16 * (number * groups + group), 16)
            value = jnp.where(chosen == number, table[pl.ds(start, 16), :].astype(F32), value)
        target[pl.ds(pl.multiple_of(at + 16 * group, 16), 16), :] = value.astype(BF16)

    def select_down(group, _):
        select(wfc2, 0, group, 4, small, 0)
        return 0

    def select_up(group, _):
        select(wfc2, up_at, group, 5, small, 64)
        return 0

    lax.fori_loop(0, 4, select_down, 0)
    lax.fori_loop(0, 5, select_up, 0)
    select(wfc2, out_down_at, 0, 1, small, 144)
    for part in range(2):
        select(act, 16 * adapters * part, 0, 1, small_hidden, 16 * part)
    for copy in give_small:
        copy.start()
    give_wout.start()
    for copy in give_small:
        copy.wait()

    @pl.when(place.swaps)
    def _():
        small[...] = wide[0:count, 3 * width : 4 * width]
        for part in range(hidden // width):
            small_hidden[:, part * width : (part + 1) * width] = wide[
                count + 32 * part : count + 32 * part + 32, 3 * width : 4 * width
            ]

    hidden_up_ref = small_hidden.at[0:16]
    hidden_down_ref = small_hidden.at[16:32]
    out_down_ref = small.at[144:160]

    def down(j):
        return small[16 * j : 16 * j + 16]

    def up(j):
        return small[64 + 16 * j : 80 + 16 * j]

    load_wfc2.start()
    give_wfc2.start()

    load_wqkv.wait()
    give_wqkv.wait_recv()

    def project(half, part):
        here = slice(half * half_rows, (half + 1) * half_rows)
        cols = slice(part * width, (part + 1) * width)
        value = dot32(x[here, :], wqkv[:, cols]) + dot32(rank_att[here, part * 16 : part * 16 + 16], up(part))
        if part == 0:
            value = (value + biases_ref[0:1, :]) * 0.125
        if part == 2:
            value = value + value_bias_ref[...]
        for two in range(peers // 2):
            turned = value[:, two * 128 : two * 128 + 128].T.astype(BF16)
            outgoing[2 * two, part * 64 : part * 64 + 64, here] = turned[0:64]
            outgoing[2 * two + 1, part * 64 : part * 64 + 64, here] = turned[64:128]

    def kv_copy(step, half):
        here = slice(half * half_rows, (half + 1) * half_rows)
        return remote(
            outgoing.at[me ^ step, 64:192, here],
            qkv.at[step, 64:192, here],
            kv_sem.at[0, half, step],
            kv_sem.at[1, half, step],
            place.peer(step),
        )

    def q_copy(step):
        return remote(
            outgoing.at[me ^ step, 0:64], qkv.at[step, 0:64], q_sem.at[0, step], q_sem.at[1, step], place.peer(step)
        )

    def back_copy(step):
        return remote(leaving.at[step], arrived.at[me], back_sem.at[0, step], back_sem.at[1, step], place.peer(step))

    steps = length // block_k
    group = block_q // rows
    key_group = block_k // rows
    for half in range(2):
        here = slice(half * half_rows, (half + 1) * half_rows)

        @pl.when(place.swaps)
        def _():
            swap_x[half].wait_recv()

        if half == 0:

            @pl.when(jnp.logical_not(place.swaps))
            def _():
                load_x.wait()

        rank_att[here, :] = dot_nt(x[here, :], small[0:48]).astype(BF16)
        project(half, 1)
        project(half, 2)
        for step in range(1, peers):
            kv_copy(step, half).start()
        project(half, 0)
    for step in range(1, peers):
        q_copy(step).start()
    give_wfc1.start()
    give_wqkv_again.start()
    load_wfc1.start()
    qkv[0] = outgoing[me]

    row_at = lax.broadcasted_iota(jnp.int32, (16, rows), 0)
    ones = (row_at == 0).astype(F32).astype(BF16)
    minus = jnp.where(lax.broadcasted_iota(jnp.int32, (rows, 16), 1) < 3, -1.0, 0.0).astype(BF16)
    minus_rows = jnp.where(lax.broadcasted_iota(jnp.int32, (64, rows), 0) < 3, -1.0, 0.0).astype(BF16)

    def tail(value):
        at = lax.broadcasted_iota(jnp.int32, (16, value.shape[1]), 0)
        high, middle, low = (part.astype(F32) for part in split_three(value))
        return jnp.where(at == 0, high, jnp.where(at == 1, middle, jnp.where(at == 2, low, 0.0))).astype(BF16)

    def take_key(turn):
        cols = pl.ds(pl.multiple_of(turn * rows, rows), rows)
        step = place.order(turn)

        @pl.when(step > 0)
        def _():
            kv_copy(step, 0).wait_recv()
            kv_copy(step, 1).wait_recv()

        key = qkv[step, 64:128, :]
        value = qkv[step, 128:192, :]
        kt[:, cols] = key
        kk[cols, 0:128] = flip(jnp.concatenate([key, key], 0))
        kk[cols, 128:144] = minus
        vv[cols, :] = flip(jnp.concatenate([value, minus_rows], 0))
        gta[0:64, cols] = value
        gta[64:80, cols] = ones
        gta[80:128, cols] = jnp.zeros((48, rows), BF16)

    def take_keys(i):
        def one(part, _):
            take_key(i * key_group + part)
            return 0

        lax.fori_loop(0, key_group, one, 0)

    def forward_part(i, low, high, arriving):
        def take_query(part, _):
            turn = i * group + part
            step = place.order(turn)
            here = pl.ds(pl.multiple_of(turn * rows, rows), rows)

            @pl.when(step > 0)
            def _():
                q_copy(step).wait_recv()

            query = qkv[step, 0:64, :].astype(F32) * LOG2E
            high = query.astype(BF16)
            qta[0:64, here] = high
            qta[64:128, here] = (query - high.astype(F32)).astype(BF16)
            return 0

        if low == 0:
            lax.fori_loop(0, group, take_query, 0)
        cols = pl.ds(pl.multiple_of(i * block_q, block_q), block_q)
        query = qta.at[0:128, cols]
        if arriving:

            @pl.when(i == 0)
            def _():
                take_keys(low)

        block = dot32(kk[low * block_k : (low + 1) * block_k, 0:128], query[...])
        big[0:block_k] = block

        def half(j, now, carry):
            peak, running, total = carry
            later = jnp.minimum(j + 1, high - 1)
            here = pl.ds(pl.multiple_of(j * block_k, block_k), block_k)
            there = pl.ds(pl.multiple_of(later * block_k, block_k), block_k)
            if arriving:

                @pl.when(jnp.logical_and(i == 0, j + 1 < high))
                def _():
                    take_keys(later)

            ahead = dot32(kk[there, 0:128], query[...])
            big[(1 - now) * block_k : (2 - now) * block_k] = ahead
            new = jnp.maximum(running, peak)
            weights = jnp.exp2(big[now * block_k : (now + 1) * block_k] - new).astype(BF16)
            total = total * jnp.exp2(running - new) + dot32(gta[0:80, here], weights)
            return jnp.max(ahead, 0, keepdims=True), new, total

        def pair(j, carry):
            return half(low + 2 * j + 1, 1, half(low + 2 * j, 0, carry))

        if low == 0:
            running, total = jnp.full((1, block_q), -jnp.inf, F32), jnp.zeros((80, block_q), F32)
        else:
            running = state[1:2, cols]
            total = jnp.concatenate([context[:, cols], state[0:1, cols], jnp.zeros((15, block_q), F32)], 0)
        _, top, total = lax.fori_loop(
            0, (high - low) // 2, pair, (jnp.max(block, 0, keepdims=True), running, total)
        )
        weight_sum = total[64:65]
        if high < steps:
            context[:, cols] = total[0:64]
            state[0:1, cols] = weight_sum
            state[1:2, cols] = top
            return
        result = total[0:64] / weight_sum
        context[:, cols] = result
        qta[128:144, cols] = tail(top + jnp.log2(weight_sum))
        low_result = result.astype(BF16)
        for part in range(group):
            step = place.order(i * group + part)
            leaving[step] = low_result[:, part * rows : (part + 1) * rows]

            @pl.when(step > 0)
            def _():
                back_copy(step).start()

    query_steps = length // block_q

    def forward_parts(first, last, low, high, arriving):
        def one(i, _):
            forward_part(i, low, high, arriving)
            return 0

        lax.fori_loop(first, last, one, 0)

    forward_parts(0, query_steps // 2, 0, steps // 2, True)
    give_wfc1.wait_recv()
    load_wfc1_far.start()
    forward_parts(0, query_steps // 2, steps // 2, steps, True)

    @pl.when(place.swaps)
    def _():
        swap_cotangent.start()

    forward_parts(query_steps // 2, query_steps, 0, steps, False)
    arrived[me] = leaving[0]

    def mean(value):
        return jnp.mean(value, -1, keepdims=True)

    def norm_backward(grad, hat, scale):
        return scale * (grad - mean(grad) - hat * mean(grad * hat))

    load_wout.wait()
    give_wout.wait_recv()
    for step in range(1, peers):
        back_copy(step).wait_recv()
    context_low = flip(arrived[...].reshape(width, rows))
    rank_out = dot_nt(context_low, out_down_ref[...]).astype(BF16)
    resid = x[...].astype(F32) + dot32(context_low, wout[...]) + biases_ref[1:2] + dot32(rank_out, up(3))
    center = resid - mean(resid)
    scale_one = lax.rsqrt(mean(center * center) + EPSILON)
    hat_one = center * scale_one
    normed = hat_one * gains_ref[0:1] + biases_ref[3:4]
    normed_low = normed.astype(BF16)
    rank_one = dot_nt(normed_low, down(3)).astype(BF16)
    load_wfc1.wait()
    load_wfc1_far.wait()
    load_wfc2.wait()
    give_wfc2.wait_recv()
    piece = 1024
    rank_two = jnp.zeros((rows, 16), F32)
    mixed = normed + biases_ref[2:3]
    for part in range(hidden // piece):
        cols = slice(part * piece, (part + 1) * piece)
        pre = (
            dot32(normed_low, wide[:, cols])
            + hidden_bias_ref[:, cols]
            + dot32(rank_one, hidden_up_ref[:, cols])
        )
        share = 0.5 + 0.5 * lax.erf(pre * 0.7071067811865476)
        big[part * rows : (part + 1) * rows] = share + pre * (0.3989422804014327 * jnp.exp(-0.5 * pre * pre))
        active = (pre * share).astype(BF16)
        act[:, cols] = active
        rank_two = rank_two + dot_nt(active, hidden_down_ref[:, cols])
        mixed = mixed + dot32(active, wfc2[cols, :])
    rank_two = rank_two.astype(BF16)
    mixed = mixed + dot32(rank_two, up(4))
    center = mixed - mean(mixed)
    scale_two = lax.rsqrt(mean(center * center) + EPSILON)
    hat_two = center * scale_two

    @pl.when(place.swaps)
    def _():
        swap_cotangent.wait_recv()

    @pl.when(jnp.logical_not(place.swaps))
    def _():
        load_cotangent.wait()

    grad_sum = norm_backward(cotangent[...].astype(F32) * gains_ref[1:2], hat_two, scale_two)
    outcome = cotangent
    outcome[...] = (hat_two * gains_ref[1:2] + biases_ref[4:5]).astype(BF16)
    home_outcome = remote(outcome, outcome_ref, swap_sem.at[0, 2], swap_sem.at[1, 2], place.partner)

    @pl.when(place.swaps)
    def _():
        home_outcome.start()

    @pl.when(jnp.logical_not(place.swaps))
    def _():
        outcome_ref[...] = outcome[...]

    grad_mixed = grad_sum.astype(BF16)
    put_term(mlp_mine, 2 * hidden, dot_tn(rank_two, grad_mixed))
    grad_rank = dot_nt(grad_mixed, up(4)).astype(BF16)
    put_term(mlp_mine, 0, dot_tn(grad_rank, act[...]))
    grad_one = jnp.zeros((rows, 16), F32)
    grad_normed = jnp.zeros((rows, width), F32)
    for part in range(hidden // piece):
        cols = slice(part * piece, (part + 1) * piece)
        grad_act = dot_nt(grad_mixed, wfc2[cols, :]) + dot32(grad_rank, hidden_down_ref[:, cols])
        grad_hidden = (grad_act.astype(BF16).astype(F32) * big[part * rows : (part + 1) * rows]).astype(BF16)
        put_term(mlp_mine, hidden + part * piece, dot_tn(rank_one, grad_hidden))
        grad_one = grad_one + dot_nt(grad_hidden, hidden_up_ref[:, cols])
        grad_normed = grad_normed + dot_nt(grad_hidden, wide[:, cols])
    grad_one = grad_one.astype(BF16)
    put_term(mlp_mine, 2 * hidden + width, dot_tn(grad_one, normed_low))
    grad_normed = (grad_normed + dot32(grad_one, down(3))).astype(BF16).astype(F32)
    resid_grad = norm_backward((grad_sum + grad_normed) * gains_ref[0:1], hat_one, scale_one)
    grad_resid = big.at[0:rows]
    grad_resid[...] = resid_grad
    grad_branch = resid_grad.astype(BF16)
    put_term(mlp_mine, 2 * hidden + 2 * width, dot_tn(rank_out, grad_branch))
    grad_rank = dot_nt(grad_branch, up(3)).astype(BF16)
    put_term(mlp_mine, 2 * hidden + 3 * width, dot_tn(grad_rank, context_low))
    turned = dot_nt(wout[...], grad_branch) + lax.dot_general(
        out_down_ref[...], grad_rank, (((0,), (1,)), ((), ())), preferred_element_type=F32
    )
    for step in range(1, peers):
        kv_copy(step, 0).wait_send()
        kv_copy(step, 1).wait_send()
        q_copy(step).wait_send()
        back_copy(step).wait_send()
    outgoing[:, 0:64] = turned.astype(BF16).reshape(peers, 64, rows)

    def grad_copy(step):
        return remote(
            outgoing.at[me ^ step, 0:64], incoming.at[step], grad_sem.at[0, step], grad_sem.at[1, step], place.peer(step)
        )

    for step in range(1, peers):
        grad_copy(step).start()
    mlp_scatter, mlp_cross, mlp_first, mlp_second, mlp_last = sum_copies(mlp_mine, mlp_parts, mlp_total, mlp_sem, place)
    incoming[0] = outgoing[me, 0:64]
    give_wqkv_again.wait_recv()
    again_wqkv.start()
    again_wqkv_far.start()
    dkv_sum[...] = jnp.zeros_like(dkv_sum)
    first = lax.broadcasted_iota(jnp.int32, (block_k, 128), 1) < 64
    dq_out = leaving

    def dq_copy(step):
        return remote(dq_out.at[step], dq_in.at[me], dq_sem.at[0, step], dq_sem.at[1, step], place.peer(step))

    def dkv_copy(step):
        return remote(dkv_out.at[step], dkv_in.at[me], dkv_sem.at[0, step], dkv_sem.at[1, step], place.peer(step))

    def backward_step(turn, _):
        last = turn == query_steps - 1
        j = (turn + query_steps // 2) % query_steps

        def take_grad(part, _):
            step = place.order(j * group + part)
            cols = pl.ds(pl.multiple_of((j * group + part) * rows, rows), rows)

            @pl.when(step > 0)
            def _():
                grad_copy(step).wait_recv()

            grad = incoming[step]
            gta[0:64, cols] = grad
            gta[64:80, cols] = tail(jnp.sum(grad.astype(F32) * context[:, cols], 0, keepdims=True))
            both[cols, :] = flip(jnp.concatenate([qkv[step, 0:64, :], grad], 0))
            return 0

        lax.fori_loop(0, group, take_grad, 0)
        cols = pl.ds(pl.multiple_of(j * block_q, block_q), block_q)

        def key_pair(pair, dq):
            found = []
            for side in range(2):
                i = (2 * pair + side + steps // 2) % steps
                here = pl.ds(pl.multiple_of(i * block_k, block_k), block_k)
                probs = jnp.exp2(dot32(kk[here, :], qta[:, cols]))
                change = dot32(vv[here, :], gta[:, cols])
                found.append((i, here, probs.astype(BF16), (probs * change).astype(BF16)))
            for i, here, probs, low in found:
                dv = dot32(probs, both[cols, :])
                dk = dot32(low, both[cols, :])
                dkv_sum[here, :] += jnp.where(first, dk, dv)
                dq = dq + dot32(kt[:, here], low)

            @pl.when(last)
            def _():
                for i, here, _, _ in found:
                    done = dkv_sum[here, :].astype(BF16)
                    for part in range(key_group):
                        step = place.order(i * key_group + part)
                        dkv_out[step] = done[part * rows : (part + 1) * rows]

                        @pl.when(step > 0)
                        def _():
                            dkv_copy(step).start()

            return dq

        dq = lax.fori_loop(0, steps // 2, key_pair, jnp.zeros((64, block_q), F32)).astype(BF16)
        for part in range(group):
            step = place.order(j * group + part)
            dq_out[step] = dq[:, part * rows : (part + 1) * rows]

            @pl.when(step > 0)
            def _():
                dq_copy(step).start()

        @pl.when(turn == query_steps // 4 - 1)
        def _():
            for copy in mlp_scatter:
                copy.start()

        @pl.when(turn == query_steps // 2 - 1)
        def _():
            sum_parts(mlp_scatter, mlp_mine, mlp_parts, mlp_total, place)
            mlp_cross.start()
            for copy in mlp_first:
                copy.start()

        @pl.when(turn == query_steps - 2)
        def _():
            mlp_cross.wait_recv()
            for copy in mlp_second:
                copy.start()

        return 0

    lax.fori_loop(0, query_steps, backward_step, 0)
    for copy in mlp_first + mlp_second:
        copy.wait_recv()
    mlp_last.start()

    def spread(total, parts):
        units = total.shape[4] // 128
        for half in range(2):
            for unit in range(peers * units):
                peer = unit // units
                lanes = slice(unit % units * 128, unit % units * 128 + 128)
                for target, low, high in parts:
                    if low <= unit * 128 < high:
                        at = unit * 128 - low
                        target(half)[:, at : at + 128] = total[(peer % 2 + half) % 2, peer // 2, half, :, lanes]

    joined = act.at[:, 0 : 3 * width]
    dq_in[me] = dq_out[0]
    dkv_in[me] = dkv_out[0]
    for step in range(1, peers):
        dkv_copy(step).wait_recv()
    left = lax.broadcasted_iota(jnp.int32, (rows, 128), 1) < 64
    for two in range(peers // 2):
        even = dkv_in[2 * two].astype(F32)
        odd = dkv_in[2 * two + 1].astype(F32)
        cols = slice(width + two * 128, width + two * 128 + 128)
        joined[:, cols] = jnp.where(left, even, pltpu.roll(odd, 64, 1)).astype(BF16)
        cols = slice(2 * width + two * 128, 2 * width + two * 128 + 128)
        joined[:, cols] = jnp.where(left, pltpu.roll(even, 64, 1), odd).astype(BF16)
    def ranks_of(part):
        grad = joined[:, part * width : (part + 1) * width]
        ranks[part] = dot_nt(grad, up(part)).astype(BF16)

    def terms_of(part):
        grad = joined[:, part * width : (part + 1) * width]
        put_term(att_mine, part * width, dot_tn(rank_att[:, part * 16 : part * 16 + 16], grad))
        put_term(att_mine, (3 + part) * width, dot_tn(ranks[part], x[...]))

    ranks = {}
    att_scatter, att_cross, att_first, att_second, att_last = sum_copies(att_mine, att_parts, att_total, att_sem, place)
    again_wqkv.wait()
    again_wqkv_far.wait()
    for part in (1, 2):
        ranks_of(part)
        terms_of(part)
    for step in range(1, peers):
        dq_copy(step).wait_recv()
    joined[:, 0:width] = (dq_in[...].reshape(width, rows).astype(F32).T * 0.125).astype(BF16)
    ranks_of(0)
    terms_of(0)
    for copy in att_scatter:
        copy.start()
    piece = width // 4
    home = [
        remote(
            grad_out.at[:, part * piece : (part + 1) * piece],
            grad_in.at[:, part * piece : (part + 1) * piece],
            swap_sem.at[0, 3 + part],
            swap_sem.at[1, 3 + part],
            place.partner,
        )
        for part in range(4)
    ]
    mlp_last.wait_recv()
    for part in range(4):
        cols = slice(part * piece, (part + 1) * piece)
        total = grad_resid[:, cols] + dot_nt(joined[...], wqkv[cols, :])
        for j in range(3):
            total = total + dot32(ranks[j], small[16 * j : 16 * j + 16, cols])
        grad_ref[:, cols] = total
        grad_out[:, cols] = total.astype(BF16)

        @pl.when(place.swaps)
        def _():
            home[part].start()

    sum_parts(att_scatter, att_mine, att_parts, att_total, place)
    att_cross.start()
    for copy in att_first:
        copy.start()
    spread(
        mlp_total,
        (
            (lambda half: hidden_down_out.at[half], 0, hidden),
            (lambda half: hidden_up_out.at[half], hidden, 2 * hidden),
            (lambda half: up_out.at[half, 4], 2 * hidden, 2 * hidden + width),
            (lambda half: down_out.at[half, 3], 2 * hidden + width, 2 * hidden + 2 * width),
            (lambda half: up_out.at[half, 3], 2 * hidden + 2 * width, 2 * hidden + 3 * width),
            (lambda half: out_down_out.at[half], 2 * hidden + 3 * width, 2 * hidden + 4 * width),
        ),
    )
    att_cross.wait_recv()
    for copy in att_second:
        copy.start()
    for copy in att_first + att_second:
        copy.wait_recv()
    att_last.start()

    @pl.when(place.swaps)
    def _():
        for part in range(4):
            home[part].wait_recv()
            cols = slice(part * piece, (part + 1) * piece)
            grad_ref[:, cols] = grad_in[:, cols].astype(F32)
        for part in range(4):
            home[part].wait_send()
        home_outcome.wait()
        for copy in swap_x:
            copy.wait_send()
        swap_cotangent.wait_send()

    att_last.wait_recv()
    spread(
        att_total,
        tuple(
            (functools.partial(lambda part, half: up_out.at[half, part], part), part * width, (part + 1) * width)
            for part in range(3)
        )
        + tuple(
            (functools.partial(lambda part, half: down_out.at[half, part], part), (3 + part) * width, (4 + part) * width)
            for part in range(3)
        ),
    )
    for step in range(1, peers):
        grad_copy(step).wait_send()
        dq_copy(step).wait_send()
        dkv_copy(step).wait_send()
    for copies in ((mlp_scatter, mlp_first, mlp_second), (att_scatter, att_first, att_second)):
        for copy in copies[0] + copies[1] + copies[2]:
            copy.wait_send()
    for copy in (mlp_cross, mlp_last, att_cross, att_last):
        copy.wait_send()
    for copy in (give_wqkv, give_wout, give_wfc2, give_wfc1, give_wqkv_again):
        copy.wait_send()
    give_chosen.wait()


def run_layer(index, tokens, cotangent, weights, tables, biases, value_bias, hidden_bias, gains):
    rows, width = tokens.shape
    peers = H
    length = peers * rows
    hidden = hidden_bias.shape[1]
    block_q, block_k = 1024, 512
    vmem = pl.BlockSpec(memory_space=pltpu.VMEM)
    hbm = pl.BlockSpec(memory_space=pl.ANY)
    mlp_part = (2 * hidden + 4 * width) // peers
    att_part = 6 * width // peers

    def out(shape, dtype=BF16):
        return jax.ShapeDtypeStruct(shape, dtype)

    def total(part):
        return pltpu.VMEM((2, peers // 2, 2, 16, part), BF16)

    def heads(*shape):
        return pltpu.VMEM((peers,) + shape, BF16)

    def sems(*shape):
        return pltpu.SemaphoreType.DMA(shape)

    return pl.pallas_call(
        functools.partial(layer_kernel, block_q, block_k),
        out_shape=[
            out((rows, width)),
            out((rows, width), F32),
            out((2, 8, 128), F32),
            out((2, 16, hidden)),
            out((2, 16, hidden)),
            out((2, 4, 16, width)),
            out((2, 5, 16, width)),
            out((2, 16, width)),
            out(weights[0].shape),
            out(weights[2].shape),
        ],
        in_specs=[pl.BlockSpec(memory_space=pltpu.SMEM)] + [hbm] * 11 + [vmem] * 4,
        out_specs=[vmem] * 8 + [hbm] * 2,
        scratch_shapes=[
            pltpu.VMEM((width, hidden), BF16),
            pltpu.VMEM((hidden, width), BF16),
            pltpu.VMEM((width, width), BF16),
            pltpu.VMEM((max(4 * rows, 2 * block_k), 1024), F32),
            pltpu.VMEM((rows, hidden), BF16),
            pltpu.VMEM((160, width), BF16),
            pltpu.VMEM((32, hidden), BF16),
            pltpu.VMEM((rows, width), BF16),
            pltpu.VMEM((rows, width), BF16),
            pltpu.VMEM((rows, 48), BF16),
            heads(192, rows),
            heads(192, rows),
            heads(64, rows),
            heads(64, rows),
            heads(64, rows),
            pltpu.VMEM((64, length), F32),
            pltpu.VMEM((8, length), F32),
            pltpu.VMEM((144, length), BF16),
            pltpu.VMEM((128, length), BF16),
            pltpu.VMEM((length, 144), BF16),
            pltpu.VMEM((length, 128), BF16),
            pltpu.VMEM((64, length), BF16),
            pltpu.VMEM((length, 128), BF16),
            pltpu.VMEM((length, 128), F32),
            heads(64, rows),
            heads(rows, 128),
            heads(rows, 128),
            pltpu.VMEM((rows, width), BF16),
            pltpu.VMEM((rows, width), BF16),
            heads(16, mlp_part),
            heads(16, mlp_part),
            total(mlp_part),
            heads(16, att_part),
            heads(16, att_part),
            total(att_part),
            sems(14),
            sems(2, 11),
            sems(2, 9),
            sems(2, 2, peers),
            sems(2, peers),
            sems(2, peers),
            sems(2, peers),
            sems(2, peers),
            sems(2, peers),
            sems(4, peers),
            sems(4, peers),
        ],
        compiler_params=pltpu.CompilerParams(
            collective_id=0, has_side_effects=True, vmem_limit_bytes=VMEM_LIMIT
        ),
        name="run_layer",
    )(index, tokens, cotangent, *weights, *tables, biases, value_bias, hidden_bias, gains)


def heads_body(
    tokens,
    cotangent,
    sequence_adapter_index,
    query_key_value_weight,
    output_weight,
    first_feed_weight,
    second_feed_weight,
    biases,
    value_bias_vector,
    first_feed_bias,
    norm_gain_pair,
    adapter_down_factors,
    output_down_factor,
    adapter_up_factors,
    hidden_up_factor,
    hidden_down_factor,
):
    width = tokens.shape[2]
    hidden = first_feed_bias.shape[0]
    adapter_number = adapter_down_factors.shape[0]
    outcome, grad_tokens, chosen, term_hd, term_uh, term_down, term_up, term_do, *_ = run_layer(
        sequence_adapter_index,
        tokens[0],
        cotangent[0],
        (query_key_value_weight, output_weight, first_feed_weight, second_feed_weight),
        (
            adapter_down_factors.reshape(-1, width),
            adapter_up_factors.reshape(-1, width),
            output_down_factor.reshape(-1, width),
            hidden_up_factor.reshape(-1, hidden),
            hidden_down_factor.reshape(-1, hidden),
        ),
        biases,
        value_bias_vector[None],
        first_feed_bias[None],
        norm_gain_pair,
    )
    tables = []
    for every in (term_down, term_do, term_up, term_uh, term_hd):
        table = 0.0
        for seq in range(2):
            mask = chosen[seq, :, 0].reshape((adapter_number,) + (1,) * (every.ndim - 1)) > 0.0
            table = table + jnp.where(mask, every[seq][None].astype(F32), 0.0)
        tables.append(table)
    return (outcome[None], grad_tokens[None], *tables)


def solution(mesh):
    one_head_each = mesh.shape["ctx"] == H and mesh.shape["fsdp"] == 2
    return jax.shard_map(
        heads_body if one_head_each else gather_body,
        mesh=mesh,
        in_specs=(
            P("fsdp", "ctx", None),
            P("fsdp", "ctx", None),
            P("fsdp"),
            P("fsdp", None),
            P("fsdp", None),
            P("fsdp", None),
            P("fsdp", None),
            P(),
            P(),
            P(),
            P(),
            P(),
            P(),
            P(),
            P(),
            P(),
        ),
        out_specs=(P("fsdp", "ctx", None), P("fsdp", "ctx", None), P(), P(), P(), P(), P()),
        check_vma=False,
    )
```

profile of v0, /device:TPU:0, one launch (start us, length us, event | category | flops | bytes accessed | tf_op | source)
XLA Modules:
  0.0 178.5 jit_solution(17708223136048492983)
XLA Ops:
  1.3 166.1 %run_layer.1 = (bf16[256,1024]{1,0:T(8,128)(2,1)}, f32[256,1024]{1,0:T(8,128)}, f32[2,8,128]{2,1,0:T(8,128)}, bf16[2,16,4096]{2,1,0:T(8,128)(2,1)}, bf16[2,16,40...) custom-call(s32[1]{0:T(128)S(6)} %copy.25.index_ref, ...), custom_call_target="tpu_custom_call" | custom-call | tf_op jit(solution)/shard_map/run_layer/pallas_call | solution.py:1190
  167.4 1.2 bitcast_convert_fusion.3
  168.6 0.8 fusion
  169.4 0.0 copy-start.2
  169.4 2.7 %select_add_fusion.1 = (f32[8,16,4096]{2,1,0:T(8,128)}, f32[8,16,4096]{2,1,0:T(8,128)}) fusion(f32[16,4096]{1,0:T(8,128)S(1)} %get-tuple-element.28, f32[16,4096]{1,0:T(8,128)S(1)} %get-tuple-element.27, pred[8]{0:T(512)(128)(4,1)S(1)} %get-tuple-element.24, pred[8]{0:T(512)(128)(4,1)S(1)} %get-tuple-element.23, f32[16,4096]{1,0:T(8,128)S(1)} %get-tuple-element.37, ...), kind=kLoop, calls=%fused_computation.1 | loop fusion | flops 3145728 | bytes 5242896 | tf_op jit(solution)/shard_map/add | solution.py:1304
  172.1 0.0 copy-done.2
  172.1 0.0 copy-start.4
  172.1 0.1 bitcast_convert_fusion.1
  172.1 0.0 copy-start.3
  172.2 1.9 %select_add_fusion = f32[8,5,16,1024]{3,2,1,0:T(8,128)} fusion(f32[5,16,1024]{2,1,0:T(8,128)S(1)} %get-tuple-element.26, f32[5,16,1024]{2,1,0:T(8,128)S(1)} %get-tuple-element.25, pred[8]{0:T(512)(128)(4,1)S(1)} %get-tuple-element.24, pred[8]{0:T(512)(128)(4,1)S(1)} %get-tuple-element.23), kind=kLoop, calls=%fused_computation | loop fusion | flops 1966080 | bytes 3276816 | tf_op jit(solution)/shard_map/add | solution.py:1304
  174.1 0.0 copy-done.4
  174.1 0.0 copy-start.1
  174.1 0.9 select_add_fusion.4
  175.0 0.0 copy-done.3
  175.0 0.0 copy-start
  175.1 1.7 select_add_fusion.3
  176.8 0.0 copy-done.1
  176.8 0.8 copy.26
  177.6 0.0 copy-done
  177.6 1.0 copy.27
  (2 shorter events, 0.1 us)
Async XLA Ops:
  169.4 2.7 %copy-start.2 = (bf16[2,5,16,1024]{3,2,1,0:T(8,128)(2,1)S(1)}, bf16[2,5,16,1024]{3,2,1,0:T(8,128)(2,1)}, u32[]{:S(2)}) copy-start(bf16[2,5,16,1024]{3,2,1,0:T(8,128)(2,1)} %get-tuple-element.20) | copy-start | bytes 983044
  172.1 2.0 %copy-start.4 = (bf16[2,16,1024]{2,1,0:T(8,128)(2,1)S(1)}, bf16[2,16,1024]{2,1,0:T(8,128)(2,1)}, u32[]{:S(2)}) copy-start(bf16[2,16,1024]{2,1,0:T(8,128)(2,1)} %get-tuple-element.19) | copy-start | bytes 196612
  172.1 2.9 %copy-start.3 = (bf16[2,4,16,1024]{3,2,1,0:T(8,128)(2,1)S(1)}, bf16[2,4,16,1024]{3,2,1,0:T(8,128)(2,1)}, u32[]{:S(2)}) copy-start(bf16[2,4,16,1024]{3,2,1,0:T(8,128)(2,1)} %get-tuple-element.18) | copy-start | bytes 786436
  174.1 2.7 %copy-start.1 = (bf16[256,1024]{1,0:T(8,128)(2,1)S(1)}, bf16[256,1024]{1,0:T(8,128)(2,1)}, u32[]{:S(2)}) copy-start(bf16[256,1024]{1,0:T(8,128)(2,1)} %get-tuple-element.15) | copy-start | bytes 1572868
  175.0 2.5 %copy-start = (f32[256,1024]{1,0:T(8,128)S(1)}, f32[256,1024]{1,0:T(8,128)}, u32[]{:S(2)}) copy-start(f32[256,1024]{1,0:T(8,128)} %get-tuple-element.16) | copy-start | bytes 3145732
where the time goes:
time: 179 us
  Pallas kernels  166 us (93%)
  other arithmetic  9.31 us (5%)
    pallas_call x1, Pallas kernels, run_layer(): pl.pallas_call(functools.partial(layer_kernel, block_q, block_k), out_sha...  166 us
    add x4, other arithmetic, heads_body(): table = table + jnp.where(mask, every[seq][None].astype(F32), 0.0)  7.21 us

commit v1 on v0

--- a/solution.py
+++ b/solution.py
@@ -1258,6 +1258,53 @@
     )(index, tokens, cotangent, *weights, *tables, biases, value_bias, hidden_bias, gains)
 
 
+def assemble_kernel(
+    chosen_ref, down_in, out_down_in, up_in, hidden_up_in, hidden_down_in, outcome_in, grad_in, outcome_out, grad_out, *tables
+):
+    sources = (down_in, out_down_in, up_in, hidden_up_in, hidden_down_in)
+    group = tables[0].shape[0]
+    for part in range(group):
+        number = pl.program_id(0) * group + part
+        masks = [chosen_ref[seq, pl.ds(number, 1), 0:1] > 0.0 for seq in range(2)]
+        for source, table in zip(sources, tables):
+            for i in range(source.shape[1]):
+                value = jnp.zeros(source.shape[2:], F32)
+                for seq, mask in enumerate(masks):
+                    value = value + jnp.where(mask, source[seq, i].astype(F32), 0.0)
+                table[part, i] = value
+    outcome_out[...] = outcome_in[...]
+    grad_out[...] = grad_in[...]
+
+
+def assemble(chosen, terms, outcome, grad_tokens):
+    adapters = chosen.shape[1]
+    steps = adapters // 2
+    block = outcome.shape[0] // steps
+    inputs = (chosen, *(term.reshape((2, -1) + term.shape[-2:]) for term in terms))
+
+    def whole(array):
+        return pl.BlockSpec(array.shape, lambda i: (0,) * array.ndim)
+
+    def part(shape):
+        return pl.BlockSpec(shape, lambda i: (i,) + (0,) * (len(shape) - 1))
+
+    rows_spec = part((block, outcome.shape[1]))
+    tables = [term.shape[1:] for term in inputs[1:]]
+    return pl.pallas_call(
+        assemble_kernel,
+        grid=(steps,),
+        out_shape=[
+            jax.ShapeDtypeStruct(outcome.shape, BF16),
+            jax.ShapeDtypeStruct(grad_tokens.shape, F32),
+            *(jax.ShapeDtypeStruct((adapters,) + shape, F32) for shape in tables),
+        ],
+        in_specs=[*(whole(array) for array in inputs), rows_spec, rows_spec],
+        out_specs=[rows_spec, rows_spec, *(part((adapters // steps,) + shape) for shape in tables)],
+        compiler_params=pltpu.CompilerParams(vmem_limit_bytes=VMEM_LIMIT),
+        name="assemble",
+    )(*inputs, outcome, grad_tokens)
+
+
 def heads_body(
     tokens,
     cotangent,
@@ -1278,7 +1325,6 @@
 ):
     width = tokens.shape[2]
     hidden = first_feed_bias.shape[0]
-    adapter_number = adapter_down_factors.shape[0]
     outcome, grad_tokens, chosen, term_hd, term_uh, term_down, term_up, term_do, *_ = run_layer(
         sequence_adapter_index,
         tokens[0],
@@ -1296,14 +1342,18 @@
         first_feed_bias[None],
         norm_gain_pair,
     )
-    tables = []
-    for every in (term_down, term_do, term_up, term_uh, term_hd):
-        table = 0.0
-        for seq in range(2):
-            mask = chosen[seq, :, 0].reshape((adapter_number,) + (1,) * (every.ndim - 1)) > 0.0
-            table = table + jnp.where(mask, every[seq][None].astype(F32), 0.0)
-        tables.append(table)
-    return (outcome[None], grad_tokens[None], *tables)
+    outcome, grad_tokens, total_down, total_out_down, total_up, total_hidden_up, total_hidden_down = assemble(
+        chosen, (term_down, term_do, term_up, term_uh, term_hd), outcome, grad_tokens
+    )
+    return (
+        outcome[None],
+        grad_tokens[None],
+        total_down,
+        total_out_down.reshape(output_down_factor.shape),
+        total_up,
+        total_hidden_up.reshape(hidden_up_factor.shape),
+        total_hidden_down.reshape(hidden_down_factor.shape),
+    )
 
 
 def solution(mesh):

time: 179 us -> 175 us (0.978)
  other arithmetic: 9.31 us -> 0 us
  Pallas kernels: 166 us -> 173 us
    add x4 -> x0, other arithmetic: 7.21 us -> none  [heads_body(): table = table + jnp.where(mask, every[seq][None].astype(F32), 0.0)]
    pallas_call x0 -> x1, Pallas kernels: none -> 6.33 us  [assemble(): pl.pallas_call(assemble_kernel, grid=(steps,), out_shape=[jax.ShapeDtypeS...]
where the time goes in v1:
time: 175 us; the launch traced here: 174 us
  Pallas kernels  173 us (99%)
    pallas_call x1, Pallas kernels, run_layer(): pl.pallas_call(functools.partial(layer_kernel, block_q, block_k), out_sha...  166 us
    pallas_call x1, Pallas kernels, assemble(): pl.pallas_call(assemble_kernel, grid=(steps,), out_shape=[jax.ShapeDtypeS...  6.33 us

profile of v1, /device:TPU:0, one launch (start us, length us, event | category | flops | bytes accessed | tf_op | source)
XLA Modules:
  0.0 174.2 jit_solution(18250849890368275434)
XLA Ops:
  1.3 166.4 %run_layer.1 = (bf16[256,1024]{1,0:T(8,128)(2,1)}, f32[256,1024]{1,0:T(8,128)}, f32[2,8,128]{2,1,0:T(8,128)}, bf16[2,16,4096]{2,1,0:T(8,128)(2,1)}, bf16[2,16,40...) custom-call(s32[1]{0:T(128)S(6)} %copy.23.index_ref, ...), custom_call_target="tpu_custom_call" | custom-call | tf_op jit(solution)/shard_map/run_layer/pallas_call | solution.py:1190
  167.7 6.3 %assemble.1 = (bf16[256,1024]{1,0:T(8,128)(2,1)}, f32[256,1024]{1,0:T(8,128)}, f32[8,4,16,1024]{3,2,1,0:T(8,128)}, f32[8,1,16,1024]{3,2,1,0:T(8,128)}, f32[8,5,1...) custom-call(f32[2,8,128]{2,1,0:T(8,128)} %get-tuple-element.22.chosen_ref, ...), custom_call_target="tpu_custom_call" | custom-call | tf_op jit(solution)/shard_map/assemble/pallas_call | solution.py:1293

commit v2 on v1

--- a/solution.py
+++ b/solution.py
@@ -951,7 +951,7 @@
 
     def backward_step(turn, _):
         last = turn == query_steps - 1
-        j = (turn + query_steps // 2) % query_steps
+        j = turn
 
         def take_grad(part, _):
             step = place.order(j * group + part)
@@ -973,7 +973,7 @@
         def key_pair(pair, dq):
             found = []
             for side in range(2):
-                i = (2 * pair + side + steps // 2) % steps
+                i = 2 * pair + side
                 here = pl.ds(pl.multiple_of(i * block_k, block_k), block_k)
                 probs = jnp.exp2(dot32(kk[here, :], qta[:, cols]))
                 change = dot32(vv[here, :], gta[:, cols])

time: 175 us -> 174 us (level)
  no operation moved by 1% of the time
where the time goes in v2:
time: 174 us; the launch traced here: 173 us
  Pallas kernels  172 us (99%)
    pallas_call x1, Pallas kernels, run_layer(): pl.pallas_call(functools.partial(layer_kernel, block_q, block_k), out_sha...  166 us
    pallas_call x1, Pallas kernels, assemble(): pl.pallas_call(assemble_kernel, grid=(steps,), out_shape=[jax.ShapeDtypeS...  6.33 us

profile of v2, /device:TPU:0, one launch (start us, length us, event | category | flops | bytes accessed | tf_op | source)
XLA Modules:
  0.0 173.5 jit_solution(6942216880167820427)
XLA Ops:
  1.3 165.7 %run_layer.1 = (bf16[256,1024]{1,0:T(8,128)(2,1)}, f32[256,1024]{1,0:T(8,128)}, f32[2,8,128]{2,1,0:T(8,128)}, bf16[2,16,4096]{2,1,0:T(8,128)(2,1)}, bf16[2,16,40...) custom-call(s32[1]{0:T(128)S(6)} %copy.23.index_ref, ...), custom_call_target="tpu_custom_call" | custom-call | tf_op jit(solution)/shard_map/run_layer/pallas_call | solution.py:1190
  167.0 6.3 %assemble.1 = (bf16[256,1024]{1,0:T(8,128)(2,1)}, f32[256,1024]{1,0:T(8,128)}, f32[8,4,16,1024]{3,2,1,0:T(8,128)}, f32[8,1,16,1024]{3,2,1,0:T(8,128)}, f32[8,5,1...) custom-call(f32[2,8,128]{2,1,0:T(8,128)} %get-tuple-element.22.chosen_ref, ...), custom_call_target="tpu_custom_call" | custom-call | tf_op jit(solution)/shard_map/assemble/pallas_call | solution.py:1293

commit v3 on v2

--- a/solution.py
+++ b/solution.py
@@ -1278,7 +1278,7 @@
 
 def assemble(chosen, terms, outcome, grad_tokens):
     adapters = chosen.shape[1]
-    steps = adapters // 2
+    steps = adapters // 4
     block = outcome.shape[0] // steps
     inputs = (chosen, *(term.reshape((2, -1) + term.shape[-2:]) for term in terms))
 

time: 174 us -> 174 us (level)
  no operation moved by 1% of the time
where the time goes in v3:
time: 174 us
  Pallas kernels  172 us (99%)
    pallas_call x1, Pallas kernels, run_layer(): pl.pallas_call(functools.partial(layer_kernel, block_q, block_k), out_sha...  166 us
    pallas_call x1, Pallas kernels, assemble(): pl.pallas_call(assemble_kernel, grid=(steps,), out_shape=[jax.ShapeDtypeS...  6.55 us

profile of v3, /device:TPU:0, one launch (start us, length us, event | category | flops | bytes accessed | tf_op | source)
XLA Modules:
  0.0 173.6 jit_solution(13317875607370032480)
XLA Ops:
  1.3 165.7 %run_layer.1 = (bf16[256,1024]{1,0:T(8,128)(2,1)}, f32[256,1024]{1,0:T(8,128)}, f32[2,8,128]{2,1,0:T(8,128)}, bf16[2,16,4096]{2,1,0:T(8,128)(2,1)}, bf16[2,16,40...) custom-call(s32[1]{0:T(128)S(6)} %copy.23.index_ref, ...), custom_call_target="tpu_custom_call" | custom-call | tf_op jit(solution)/shard_map/run_layer/pallas_call | solution.py:1190
  167.0 6.5 %assemble.1 = (bf16[256,1024]{1,0:T(8,128)(2,1)}, f32[256,1024]{1,0:T(8,128)}, f32[8,4,16,1024]{3,2,1,0:T(8,128)}, f32[8,1,16,1024]{3,2,1,0:T(8,128)}, f32[8,5,1...) custom-call(f32[2,8,128]{2,1,0:T(8,128)} %get-tuple-element.22.chosen_ref, ...), custom_call_target="tpu_custom_call" | custom-call | tf_op jit(solution)/shard_map/assemble/pallas_call | solution.py:1293
